TPU v7x, 512 devices: a whole 4x4x16 slice. The times are simulated.
512 devices in a mesh: dp: 16 (over z_lo, core), code: 32 (over z_hi, y, x).
Axes of the slice: x: 4, y: 4, z: 16 (z_hi: 2, z_lo: 8; z = z_hi * 8 + z_lo), core: 2. Of those that a mesh axis runs over, the one named last changes fastest.
Arguments:
- latents: bfloat16 [16384, 256], P('dp'), may hold values from -30 to 30
- codebook: bfloat16 [131072, 256], P('code'), may hold values from -6 to 6
- old_counts: float32 [131072], P('code'), may hold values from 0.002 to 0.02
- old_sums: float32 [256, 131072], P('dp', 'code'), may hold values from -0.06 to 0.06
Outputs:
- quantized: bfloat16 [16384, 256], P('dp')
- counts_next: float32 [131072], P('code')
- codebook_next: float32 [256, 131072], P('dp', 'code')
All inputs are finite; a program needn't handle non-finite values.
Results may differ from a plain program's by a relative error of at most 0.0043.
Values may be sent and summed in bfloat16 or wider, within the bound.
A program may use at most 64 MiB of HBM per device.

v0:
```python
import math

import jax
import jax.numpy as jnp
from jax import lax
from jax.sharding import PartitionSpec as P


def against_codes(row_block, codebook):
    return lax.dot_general(
        row_block, codebook, (((1,), (1,)), ((), ())), preferred_element_type=jnp.float32
    )


def over_rows(left_rows, right_rows):
    return lax.dot_general(
        left_rows, right_rows, (((0,), (0,)), ((), ())), preferred_element_type=jnp.float32
    )


def body(latents, codebook, old_counts, old_sums):
    rows_dev = latents.shape[0]
    width = latents.shape[1]
    block_rows = min(512, rows_dev)
    logit_scale = 2.0 / math.sqrt(width)
    code_norms = jnp.sum(jnp.square(codebook.astype(jnp.float32)), axis=1)
    weight_blocks = []
    for index_block in range(rows_dev // block_rows):
        row_block = latents[index_block * block_rows : (index_block + 1) * block_rows]
        logits = (2.0 * against_codes(row_block, codebook) - code_norms[None, :]) * logit_scale
        row_top = lax.pmax(jnp.max(logits, axis=1), "code")
        raised = jnp.exp(logits - row_top[:, None])
        row_total = lax.psum(jnp.sum(raised, axis=1), "code")
        weight_block = (raised / row_total[:, None]).astype(jnp.bfloat16)
        weight_blocks.append(weight_block)
    weights = jnp.concatenate(weight_blocks, axis=0)
    partial_quant = jnp.dot(weights, codebook, preferred_element_type=jnp.float32)
    quantized = lax.psum(partial_quant, "code").astype(jnp.bfloat16)
    ones_row = jnp.ones((1, rows_dev), jnp.bfloat16)
    local_counts = jnp.dot(ones_row, weights, preferred_element_type=jnp.float32)[0]
    counts = lax.psum(local_counts, "dp")
    stat_term = over_rows(latents, weights)
    code_sums = lax.psum_scatter(
        stat_term.astype(jnp.bfloat16), "dp", scatter_dimension=0, tiled=True
    ).astype(jnp.float32)
    counts_next = 0.9 * old_counts + 0.1 * counts
    sums_next = 0.9 * old_sums + 0.1 * code_sums
    codebook_next = sums_next / counts_next[None, :]
    return (quantized, counts_next, codebook_next)


def solution(mesh):
    return jax.shard_map(
        body,
        mesh=mesh,
        in_specs=(P("dp", None), P("code", None), P("code"), P("dp", "code")),
        out_specs=(P("dp", None), P("code"), P("dp", "code")),
        check_vma=False,
    )
```

profile of v0, /device:TPU:0, one launch (start us, length us, event | category | flops | bytes accessed | tf_op | source)
XLA Modules:
  0.0 766.0 jit_solution(15042874151414876809)
XLA Ops:
  7.2 0.0 copy-start.5
  7.2 0.0 copy-start.9
  7.2 0.0 reduce-scatter.4.cloned.1.call-start
  7.2 2.4 multiply_reduce_fusion
  9.6 6.2 fusion.12
  15.8 0.0 copy-done.5
  15.8 0.0 copy-done.9
  15.8 4.5 fusion.13
  20.4 159.6 %all-reduce.1 = (f32[512]{0:T(512)S(1)}, f32[512]{0:T(512)S(1)}) all-reduce(f32[512]{0:T(512)S(1)} %get-tuple-element.13, f32[512]{0:T(512)S(1)} %get-tuple-element.15), channel_id=1, replica_groups=mesh['dp'=16,'code'=32] {'code'}, use_global_device_ids=true, to_apply=%region_6.0 | all-reduce | flops 1024 | bytes 8192 | tf_op jit(solution)/shard_map/pmax | solution.py:31
  179.9 0.0 copy-start
  180.0 4.8 fusion.1
  184.7 1.0 copy-done
  185.7 1.3 fusion
  187.0 146.7 %all-reduce = (f32[512]{0:T(512)S(1)}, f32[512]{0:T(512)S(1)}) all-reduce(f32[512]{0:T(512)S(1)} %fusion.1, f32[512]{0:T(512)S(1)} %fusion), channel_id=1, replica_groups=mesh['dp'=16,'code'=32] {'code'}, use_global_device_ids=true, to_apply=%region_8.0 | all-reduce | flops 1024 | bytes 8192 | tf_op jit(solution)/shard_map/psum | solution.py:33
  333.7 8.0 %divide_convert_fusion = (bf16[512,4096]{1,0:T(8,128)(2,1)S(1)}, bf16[512,4096]{1,0:T(8,128)(2,1)S(1)}) fusion(f32[512,4096]{1,0:T(8,128)} %get-tuple-element.14, f32[512]{0:T(512)S(1)} %get-tuple-element.9, f32[512]{0:T(512)S(1)} %get-tuple-element.11, f32[512]{0:T(512)S(1)} %get-tuple-element.10, f32[512,4096]{1,0:T(8,128)} %get-tuple-element.16, ...), kind=kLoop, calls=%fused_computation.1 | loop fusion | flops 12582912 | bytes 25174016 | tf_op jit(solution)/shard_map/convert_element_type | solution.py:34
  341.7 0.0 copy-start.1
  341.7 0.0 copy-start.3
  341.7 1.9 copy-done.1
  343.6 1.3 copy-done.3
  344.9 3.7 fusion.2
  348.6 4.1 copy.14
  352.7 0.0 reduce-scatter.4.cloned.1.call-update
  352.7 0.0 copy-start.2
  352.7 0.0 copy-start.4
  352.7 5.9 fusion.4
  358.6 0.0 copy-done.2
  358.7 0.0 copy-done.4
  358.7 0.0 copy-start.8
  358.7 0.0 copy-start.6
  358.7 1.3 fusion.3
  360.0 90.1 %psum.31 = f32[4096]{0:T(1024)S(1)} all-reduce(f32[4096]{0:T(1024)S(1)} %bitcast.8), channel_id=1, replica_groups=mesh['dp'=16,'code'=32] {'dp'}, use_global_device_ids=true, to_apply=%region_10.0 | all-reduce | flops 4096 | bytes 32768 | tf_op jit(solution)/shard_map/psum | solution.py:41
  450.1 0.0 copy-done.8
  450.1 0.0 copy-start.7
  450.1 307.3 %all-reduce.3 = bf16[1024,256]{1,0:T(8,128)(2,1)} all-reduce(f32[1024,256]{1,0:T(8,128)S(1)} %fusion.4), channel_id=1, replica_groups=mesh['dp'=16,'code'=32] {'code'}, use_global_device_ids=true, to_apply=%region_9.0 | all-reduce | flops 262144 | bytes 1572864 | tf_op jit(solution)/shard_map/psum | solution.py:38
  757.5 0.0 reduce-scatter.4.cloned.1.call-done
  757.5 0.0 copy-done.6
  757.5 1.7 add_divide_fusion
  759.1 0.0 copy-done.7
  (1 shorter events, 0.0 us)
Async XLA Ops:
  7.2 8.7 %copy-start.5 = (bf16[4096,256]{1,0:T(8,128)(2,1)S(1)}, bf16[4096,256]{1,0:T(8,128)(2,1)}, u32[]{:S(2)}) copy-start(bf16[4096,256]{1,0:T(8,128)(2,1)} %param.5) | copy-start | bytes 6291460
  7.2 8.7 %copy-start.9 = (bf16[1024,256]{1,0:T(8,128)(2,1)S(1)}, bf16[1024,256]{1,0:T(8,128)(2,1)}, u32[]{:S(2)}) copy-start(bf16[1024,256]{1,0:T(8,128)(2,1)} %param.4) | copy-start | bytes 1572868
  7.2 750.3 %reduce-scatter.4.cloned.1.call-start = ((), (), s32[]{:S(2)}) async-start(), calls=%async_computation.1 | async-start | bytes 2228224 | tf_op jit(solution)/shard_map/reduce_scatter | solution.py:43
  179.9 5.8 copy-start
  341.7 1.9 copy-start.1
  341.7 3.2 copy-start.3
  352.7 6.0 copy-start.2
  352.7 6.0 copy-start.4
  358.7 91.5 %copy-start.8 = (f32[4096]{0:T(1024)S(1)}, f32[4096]{0:T(1024)}, u32[]{:S(2)}) copy-start(f32[4096]{0:T(1024)} %param.6) | copy-start | bytes 49156
  358.7 398.8 %copy-start.6 = (f32[16,4096]{1,0:T(8,128)S(1)}, f32[16,4096]{1,0:T(8,128)}, u32[]{:S(2)}) copy-start(f32[16,4096]{1,0:T(8,128)} %param.7) | copy-start | bytes 786436
  450.1 309.0 %copy-start.7 = (f32[4096]{0:T(1024)}, f32[4096]{0:T(1024)S(1)}, u32[]{:S(2)}) copy-start(f32[4096]{0:T(1024)S(1)} %multiply_add_fusion) | copy-start | bytes 49156
Sparse Core Ops, SparseCore 0:
  352.8 100.0 reduce-scatter.3
where the time goes:
time: 766 us
  blocking collectives  704 us (92%)
  matrix products  21.7 us (3%)
  other arithmetic  18 us (2%)
  between operations  14.1 us (2%)
  local copies, waits for them, and re-layouts  8.33 us (1%)
    psum x1, blocking collectives, body(): quantized = lax.psum(partial_quant, 'code').astype(jnp.bfloat16)  307 us
    pmax x1, blocking collectives, body(): row_top = lax.pmax(jnp.max(logits, axis=1), 'code')  160 us
    psum x1, blocking collectives, body(): row_total = lax.psum(jnp.sum(raised, axis=1), 'code')  147 us
    psum x1, blocking collectives, body(): counts = lax.psum(local_counts, 'dp')  90.1 us
  transfers between devices with their start and end apart: 1, of which 0 were waited for; matrix products, arithmetic and copies ran while one was open for 1% of the time, Pallas kernels for 0%

commit v1 on v0

v1 whole, which is shorter than its diff:
```python
import math

import jax
import jax.numpy as jnp
from jax import lax
from jax.experimental import pallas as pl
from jax.experimental.pallas import tpu as pltpu
from jax.sharding import PartitionSpec as P

MESH = pl.DeviceIdType.MESH
F32 = jnp.float32
BF16 = jnp.bfloat16

ROWS = 1024
CODES = 4096
WIDTH = 256
BLOCK = 512
BLOCKS = CODES // BLOCK
PLANE = 16
PIECE = WIDTH // PLANE
LINE = 8
SUBS = 4
SUB = CODES // SUBS
SHARE = 16
HALF = SHARE * LINE


def dot(a, b):
    return lax.dot_general(a, b, (((1,), (0,)), ((), ())), preferred_element_type=F32)


def dot_t(a, b):
    return lax.dot_general(a, b, (((1,), (1,)), ((), ())), preferred_element_type=F32)


def kernel(
    latents_hbm, codebook_hbm, old_counts_ref, old_sums_ref,
    quant_ref, counts_ref, next_ref,
    lat, lat_t, code, code_t, logits, raised,
    stat_in, zstat_out, zstat_in,
    q_acc, q_send, q_in, zq_out, zq_in, q_all,
    scaled, own, pair_out, pair_in, cnt, cnt_pair, cnt_right, cnt_left, cnt_to_right, cnt_to_left,
    right_in, left_in, right_out, left_out,
    lat_sem, code_sem,
    stat_s, stat_r, zstat_sem, q_s, q_r, zq_sem, qa_s, qa_r,
    pair_s, pair_r, cntp_sem, cntr_sem, cntl_sem, right_s, right_r, left_s, left_r,
):
    dp = lax.axis_index("dp")
    cd = lax.axis_index("code")
    z = dp // 2
    core = dp % 2
    zh = cd // PLANE
    xy = cd % PLANE
    partner = (dp + 1 - 2 * core, cd)
    across = (dp, (1 - zh) * PLANE + xy)

    def peer(i):
        j = (xy + i) % PLANE
        return j, (dp, zh * PLANE + j)

    lat_copy = pltpu.make_async_copy(latents_hbm, lat, lat_sem)
    lat_copy.start()

    def code_copy(b):
        rows = pl.ds(pl.multiple_of(b * BLOCK, BLOCK), BLOCK)
        return pltpu.make_async_copy(codebook_hbm.at[rows], code.at[rows], code_sem.at[b])

    for b in range(BLOCKS):
        code_copy(b).start()

    barrier = pltpu.get_barrier_semaphore()

    def greet(i, carry):
        pl.semaphore_signal(barrier, inc=1, device_id=peer(i)[1], device_id_type=MESH)
        return carry

    lax.fori_loop(1, PLANE, greet, 0)
    pl.semaphore_signal(barrier, inc=1, device_id=partner, device_id_type=MESH)
    pl.semaphore_signal(barrier, inc=1, device_id=across, device_id_type=MESH)

    @pl.when(z > 0)
    def _():
        pl.semaphore_signal(barrier, inc=1, device_id=(dp - 2, cd), device_id_type=MESH)

    @pl.when(z < LINE - 1)
    def _():
        pl.semaphore_signal(barrier, inc=1, device_id=(dp + 2, cd), device_id_type=MESH)

    lat_copy.wait()
    lat_t[...] = lat[...].T

    per_dot = 2.0 * 2.0 / math.sqrt(WIDTH) * math.log2(math.e)
    per_norm = 2.0 / math.sqrt(WIDTH) * math.log2(math.e)

    def first(b, top):
        code_copy(b).wait()
        rows = pl.ds(pl.multiple_of(b * BLOCK, BLOCK), BLOCK)
        block = code[rows, :]
        wide = block.astype(F32)
        norms = jnp.sum(wide * wide, axis=1, keepdims=True) * per_norm
        part = dot(block, lat_t[...]) * per_dot - norms
        logits[rows, :] = part
        code_t[:, rows] = block.T
        return jnp.maximum(top, jnp.max(part.reshape(BLOCK // 8, 8, ROWS), axis=0))

    top = lax.fori_loop(0, BLOCKS, first, jnp.full((8, ROWS), -jnp.inf, F32))
    top = jnp.max(top, axis=0, keepdims=True)

    q_acc[...] = jnp.zeros_like(q_acc)

    def second(b, total):
        rows = pl.ds(pl.multiple_of(b * BLOCK, BLOCK), BLOCK)
        part = jnp.exp2(logits[rows, :] - top)
        low = part.astype(BF16)
        raised[rows, :] = low
        q_acc[...] += dot(code_t[:, rows], low)
        return total + jnp.sum(part.reshape(BLOCK // 8, 8, ROWS), axis=0)

    total = lax.fori_loop(0, BLOCKS, second, jnp.zeros((8, ROWS), F32))
    total = jnp.sum(total, axis=0, keepdims=True)

    stat_in[xy, 0:1, :] = top
    stat_in[xy, 1:2, :] = total
    ends = (z == 0) | (z == LINE - 1)

    @pl.when(ends)
    def _():
        pl.semaphore_wait(barrier, PLANE + 2)

    @pl.when(jnp.logical_not(ends))
    def _():
        pl.semaphore_wait(barrier, PLANE + 3)

    def stat_copy(i):
        j, device = peer(i)
        return pltpu.make_async_remote_copy(
            stat_in.at[xy], stat_in.at[xy], stat_s.at[i], stat_r.at[xy], device_id=device, device_id_type=MESH)

    def stat_wait(i):
        j, device = peer(i)
        pltpu.make_async_remote_copy(
            stat_in.at[j], stat_in.at[j], stat_s.at[i], stat_r.at[j], device_id=device, device_id_type=MESH).wait_recv()

    def each(run):
        def step(i, carry):
            run(i)
            return carry
        lax.fori_loop(1, PLANE, step, 0)

    each(lambda i: stat_copy(i).start())

    q_send[...] = q_acc[...].astype(BF16)

    def piece(j):
        return pl.ds(pl.multiple_of(j * PIECE, PIECE), PIECE)

    def q_copy(i):
        j, device = peer(i)
        return pltpu.make_async_remote_copy(
            q_send.at[piece(j)], q_in.at[xy], q_s.at[i], q_r.at[xy], device_id=device, device_id_type=MESH)

    def q_wait(i):
        j, device = peer(i)
        pltpu.make_async_remote_copy(
            q_send.at[piece(j)], q_in.at[j], q_s.at[i], q_r.at[j], device_id=device, device_id_type=MESH).wait_recv()

    each(lambda i: q_copy(i).start())
    q_in[xy] = q_send[piece(xy), :]

    each(stat_wait)
    plane_top = stat_in[0, 0:1, :]
    for j in range(1, PLANE):
        plane_top = jnp.maximum(plane_top, stat_in[j, 0:1, :])
    plane_total = jnp.zeros((1, ROWS), F32)
    for j in range(PLANE):
        plane_total += stat_in[j, 1:2, :] * jnp.exp2(stat_in[j, 0:1, :] - plane_top)
    zstat_out[0:1, :] = plane_top
    zstat_out[1:2, :] = plane_total
    zstat_copy = pltpu.make_async_remote_copy(
        zstat_out, zstat_in, zstat_sem.at[0], zstat_sem.at[1], device_id=across, device_id_type=MESH)
    zstat_copy.start()

    each(q_wait)
    plane_q = jnp.zeros((PIECE, ROWS), F32)
    for j in range(PLANE):
        plane_q += q_in[j].astype(F32) * jnp.exp2(stat_in[j, 0:1, :] - plane_top)
    zq_out[...] = plane_q.astype(BF16)
    zq_copy = pltpu.make_async_remote_copy(
        zq_out, zq_in, zq_sem.at[0], zq_sem.at[1], device_id=across, device_id_type=MESH)
    zq_copy.start()

    zstat_copy.wait_recv()
    other_top = zstat_in[0:1, :]
    full_top = jnp.maximum(plane_top, other_top)
    mine_factor = jnp.exp2(plane_top - full_top)
    other_factor = jnp.exp2(other_top - full_top)
    full_total = plane_total * mine_factor + zstat_in[1:2, :] * other_factor
    inverse = 1.0 / full_total
    factor = jnp.exp2(top - full_top) * inverse

    for side in range(2):
        which = core if side == 0 else 1 - core
        for c in range(LINE):
            src = pl.ds(pl.multiple_of(c * 2 * SHARE + which * SHARE, SHARE), SHARE)
            scaled[side * HALF + c * SHARE : side * HALF + (c + 1) * SHARE, :] = (
                lat_t[src, :].astype(F32) * factor).astype(BF16)
    high = factor.astype(BF16)
    rest = (factor - high.astype(F32)).astype(BF16)
    line_no = lax.broadcasted_iota(jnp.int32, (SHARE, ROWS), 0)
    scaled[WIDTH : WIDTH + SHARE, :] = jnp.where(
        line_no == 0, high.astype(F32), jnp.where(line_no == 1, rest.astype(F32), 0.0)).astype(BF16)

    def sub(q):
        return pl.ds(q * SUB, SUB)

    def pair_copy(q):
        return pltpu.make_async_remote_copy(
            pair_out.at[:, sub(q)], pair_in.at[:, sub(q)], pair_s.at[q], pair_r.at[q],
            device_id=partner, device_id_type=MESH)

    for q in range(SUBS):
        sums = dot_t(scaled[...], raised[sub(q), :])
        pair_out[:, sub(q)] = sums[HALF:WIDTH].astype(BF16)
        pair_copy(q).start()
        own[:, sub(q)] = sums[0:HALF]
        cnt[:, sub(q)] = sums[WIDTH : WIDTH + 1] + sums[WIDTH + 1 : WIDTH + 2]

    cntp_copy = pltpu.make_async_remote_copy(
        cnt, cnt_pair, cntp_sem.at[0], cntp_sem.at[1], device_id=partner, device_id_type=MESH)
    cntp_copy.start()

    def right_copy(t, q):
        return pltpu.make_async_remote_copy(
            right_out.at[t, :, sub(q)], right_in.at[t, :, sub(q)], right_s.at[t, q], right_r.at[t, q],
            device_id=(dp + 2, cd), device_id_type=MESH)

    def left_copy(t, q):
        return pltpu.make_async_remote_copy(
            left_out.at[t, :, sub(q)], left_in.at[t, :, sub(q)], left_s.at[t, q], left_r.at[t, q],
            device_id=(dp - 2, cd), device_id_type=MESH)

    def share(c):
        return pl.ds(pl.multiple_of(c * SHARE, SHARE), SHARE)

    last = LINE - 1

    def right_step(t, q):
        @pl.when(t >= z)
        def _():
            mine = own[share(last - t + z), sub(q)]
            if t == 0:
                right_out[t, :, sub(q)] = mine.astype(BF16)
            else:
                @pl.when(z > 0)
                def _():
                    right_copy(t - 1, q).wait_recv()
                    right_out[t, :, sub(q)] = (mine + right_in[t - 1, :, sub(q)].astype(F32)).astype(BF16)

                @pl.when(z == 0)
                def _():
                    right_out[t, :, sub(q)] = mine.astype(BF16)
            right_copy(t, q).start()

    def left_step(t, q):
        @pl.when(t >= last - z)
        def _():
            mine = own[share(t - last + z), sub(q)]
            if t == 0:
                left_out[t, :, sub(q)] = mine.astype(BF16)
            else:
                @pl.when(z < last)
                def _():
                    left_copy(t - 1, q).wait_recv()
                    left_out[t, :, sub(q)] = (mine + left_in[t - 1, :, sub(q)].astype(F32)).astype(BF16)

                @pl.when(z == last)
                def _():
                    left_out[t, :, sub(q)] = mine.astype(BF16)
            left_copy(t, q).start()

    cntr_copy = pltpu.make_async_remote_copy(
        cnt_to_right, cnt_right, cntr_sem.at[0], cntr_sem.at[1], device_id=(dp + 2, cd), device_id_type=MESH)
    cntl_copy = pltpu.make_async_remote_copy(
        cnt_to_left, cnt_left, cntl_sem.at[0], cntl_sem.at[1], device_id=(dp - 2, cd), device_id_type=MESH)

    for t in range(last):
        for q in range(SUBS):
            if t == 0:
                pair_copy(q).wait_recv()
                own[:, sub(q)] += pair_in[:, sub(q)].astype(F32)
            right_step(t, q)
            left_step(t, q)
        if t == 0:
            cntp_copy.wait_recv()
            cnt_pair[...] += cnt[...]

            zq_copy.wait_recv()
            share_q = (plane_q * mine_factor + zq_in[...].astype(F32) * other_factor) * inverse
            q_all[xy] = share_q.astype(BF16)

            def qa_copy(i):
                j, device = peer(i)
                return pltpu.make_async_remote_copy(
                    q_all.at[xy], q_all.at[xy], qa_s.at[i], qa_r.at[xy], device_id=device, device_id_type=MESH)

            def qa_wait(i):
                j, device = peer(i)
                pltpu.make_async_remote_copy(
                    q_all.at[j], q_all.at[j], qa_s.at[i], qa_r.at[j], device_id=device, device_id_type=MESH).wait_recv()

            each(lambda i: qa_copy(i).start())

        @pl.when(t == z)
        def _():
            if t == 0:
                cnt_to_right[...] = cnt_pair[...]
            else:
                cntr_copy.wait_recv()
                cnt_to_right[...] = cnt_pair[...] + cnt_right[...]
            cntr_copy.start()

        @pl.when(t == last - z)
        def _():
            if t == 0:
                cnt_to_left[...] = cnt_pair[...]
            else:
                cntl_copy.wait_recv()
                cnt_to_left[...] = cnt_pair[...] + cnt_left[...]
            cntl_copy.start()

    each(qa_wait)
    quant_ref[...] = q_all[...].reshape(WIDTH, ROWS).T

    @pl.when(z == 0)
    def _():
        cntl_copy.wait_recv()
        counts_ref[...] = cnt_pair[...] + cnt_left[...]

    @pl.when(z == last)
    def _():
        cntr_copy.wait_recv()
        counts_ref[...] = cnt_pair[...] + cnt_right[...]

    @pl.when((z > 0) & (z < last))
    def _():
        counts_ref[...] = cnt_pair[...] + cnt_left[...] + cnt_right[...]

    counts_ref[...] = 0.9 * old_counts_ref[...] + 0.1 * counts_ref[...]

    for q in range(SUBS):
        @pl.when(z > 0)
        def _():
            right_copy(last - 1, q).wait_recv()
            own[share(z), sub(q)] += right_in[last - 1, :, sub(q)].astype(F32)

        @pl.when(z < last)
        def _():
            left_copy(last - 1, q).wait_recv()
            own[share(z), sub(q)] += left_in[last - 1, :, sub(q)].astype(F32)

        sums_next = 0.9 * old_sums_ref[:, sub(q)] + 0.1 * own[share(z), sub(q)]
        next_ref[:, sub(q)] = sums_next / counts_ref[:, sub(q)]

    each(lambda i: stat_copy(i).wait_send())
    each(lambda i: q_copy(i).wait_send())
    each(lambda i: qa_copy(i).wait_send())
    zstat_copy.wait_send()
    zq_copy.wait_send()
    cntp_copy.wait_send()
    for q in range(SUBS):
        pair_copy(q).wait_send()

    @pl.when(z < last)
    def _():
        cntr_copy.wait_send()

    @pl.when(z > 0)
    def _():
        cntl_copy.wait_send()

    for t in range(last):
        @pl.when(t >= z)
        def _():
            for q in range(SUBS):
                right_copy(t, q).wait_send()

        @pl.when(t >= last - z)
        def _():
            for q in range(SUBS):
                left_copy(t, q).wait_send()


def body(latents, codebook, old_counts, old_sums):
    any_spec = pl.BlockSpec(memory_space=pl.ANY)
    vmem_spec = pl.BlockSpec(memory_space=pltpu.VMEM)
    dma = pltpu.SemaphoreType.DMA
    quantized, counts_next, codebook_next = pl.pallas_call(
        kernel,
        out_shape=(
            jax.ShapeDtypeStruct((ROWS, WIDTH), BF16),
            jax.ShapeDtypeStruct((1, CODES), F32),
            jax.ShapeDtypeStruct((SHARE, CODES), F32),
        ),
        in_specs=[any_spec, any_spec, vmem_spec, vmem_spec],
        out_specs=(vmem_spec, vmem_spec, vmem_spec),
        scratch_shapes=[
            pltpu.VMEM((ROWS, WIDTH), BF16),
            pltpu.VMEM((WIDTH, ROWS), BF16),
            pltpu.VMEM((CODES, WIDTH), BF16),
            pltpu.VMEM((WIDTH, CODES), BF16),
            pltpu.VMEM((CODES, ROWS), F32),
            pltpu.VMEM((CODES, ROWS), BF16),
            pltpu.VMEM((PLANE, 2, ROWS), F32),
            pltpu.VMEM((2, ROWS), F32),
            pltpu.VMEM((2, ROWS), F32),
            pltpu.VMEM((WIDTH, ROWS), F32),
            pltpu.VMEM((WIDTH, ROWS), BF16),
            pltpu.VMEM((PLANE, PIECE, ROWS), BF16),
            pltpu.VMEM((PIECE, ROWS), BF16),
            pltpu.VMEM((PIECE, ROWS), BF16),
            pltpu.VMEM((PLANE, PIECE, ROWS), BF16),
            pltpu.VMEM((WIDTH + SHARE, ROWS), BF16),
            pltpu.VMEM((HALF, CODES), F32),
            pltpu.VMEM((HALF, CODES), BF16),
            pltpu.VMEM((HALF, CODES), BF16),
            pltpu.VMEM((1, CODES), F32),
            pltpu.VMEM((1, CODES), F32),
            pltpu.VMEM((1, CODES), F32),
            pltpu.VMEM((1, CODES), F32),
            pltpu.VMEM((1, CODES), F32),
            pltpu.VMEM((1, CODES), F32),
            pltpu.VMEM((LINE - 1, SHARE, CODES), BF16),
            pltpu.VMEM((LINE - 1, SHARE, CODES), BF16),
            pltpu.VMEM((LINE - 1, SHARE, CODES), BF16),
            pltpu.VMEM((LINE - 1, SHARE, CODES), BF16),
            dma,
            dma((BLOCKS,)),
            dma((PLANE,)),
            dma((PLANE,)),
            dma((2,)),
            dma((PLANE,)),
            dma((PLANE,)),
            dma((2,)),
            dma((PLANE,)),
            dma((PLANE,)),
            dma((SUBS,)),
            dma((SUBS,)),
            dma((2,)),
            dma((2,)),
            dma((2,)),
            dma((LINE - 1, SUBS)),
            dma((LINE - 1, SUBS)),
            dma((LINE - 1, SUBS)),
            dma((LINE - 1, SUBS)),
        ],
        compiler_params=pltpu.CompilerParams(
            collective_id=0, has_side_effects=True, vmem_limit_bytes=60 * 1024 * 1024),
        cost_estimate=pl.CostEstimate(flops=6_500_000_000, bytes_accessed=4_000_000, transcendentals=4_200_000),
    )(latents, codebook, old_counts.reshape(1, CODES), old_sums)
    return quantized, counts_next.reshape(CODES), codebook_next


def solution(mesh):
    return jax.shard_map(
        body,
        mesh=mesh,
        in_specs=(P("dp", None), P("code", None), P("code"), P("dp", "code")),
        out_specs=(P("dp", None), P("code"), P("dp", "code")),
        check_vma=False,
    )
```

time: 766 us -> 74.4 us (0.10)
  the two profiles are of different devices: /device:TPU:0 before, /device:TPU:2 now
where the time goes in v1:
time: 74.4 us; the launch traced here: 74.1 us
  Pallas kernels  68.6 us (92%)
  local copies, waits for them, and re-layouts  4.86 us (7%)
    pallas_call x1, Pallas kernels, body(): pl.pallas_call(kernel, out_shape=(jax.ShapeDtypeStruct((ROWS, WIDTH), BF1...  68.6 us
    unnamed x3, local copies, waits for them, and re-layouts  4.86 us

profile of v1, /device:TPU:2, one launch (start us, length us, event | category | flops | bytes accessed | tf_op | source)
XLA Modules:
  0.0 74.1 jit_solution(4840835938605859849)
XLA Ops:
  0.6 68.6 %shard_map.67 = (bf16[1024,256]{1,0:T(8,128)(2,1)}, f32[1,4096]{1,0:T(1,128)}, f32[16,4096]{1,0:T(8,128)}) custom-call(bf16[1024,256]{1,0:T(8,128)(2,1)} %latents_hbm.1, bf16[4096,256]{1,0:T(8,128)(2,1)} %codebook_hbm.1, f32[1,4096]{1,0:T(1,128)} %bitcast.3, f32[16,4096]{1,0:T(8,128)} %old_sums_ref.1), custom_call_target="tpu_custom_call" | custom-call | flops 6499999744 | bytes 4000000 | tf_op jit(solution)/shard_map/pallas_call | solution.py:397
  69.2 1.9 %copy.10 = bf16[1024,256]{1,0:T(8,128)(2,1)} copy(bf16[1024,256]{1,0:T(8,128)(2,1)} %get-tuple-element.12) | data formatting | bytes 1048576
  71.1 1.3 %copy.11 = f32[4096]{0:T(1024)} copy(f32[4096]{0:T(1024)} %bitcast.2) | data formatting | bytes 32768
  72.4 1.7 %copy.12 = f32[16,4096]{1,0:T(8,128)} copy(f32[16,4096]{1,0:T(8,128)} %get-tuple-element.14) | data formatting | bytes 524288

commit v2 on v1

--- a/solution.py
+++ b/solution.py
@@ -34,11 +34,10 @@
 
 
 def kernel(
-    latents_hbm, codebook_hbm, old_counts_ref, old_sums_ref,
-    quant_ref, counts_ref, next_ref,
+    latents_hbm, codebook_hbm, quant_ref, counts_ref, sums_ref,
     lat, lat_t, code, code_t, logits, raised,
     stat_in, zstat_out, zstat_in,
-    q_acc, q_send, q_in, zq_out, zq_in, q_all,
+    q_part, q_send, q_in, zq_out, zq_in, q_all,
     scaled, own, pair_out, pair_in, cnt, cnt_pair, cnt_right, cnt_left, cnt_to_right, cnt_to_left,
     right_in, left_in, right_out, left_out,
     lat_sem, code_sem,
@@ -106,21 +105,17 @@
     top = lax.fori_loop(0, BLOCKS, first, jnp.full((8, ROWS), -jnp.inf, F32))
     top = jnp.max(top, axis=0, keepdims=True)
 
-    q_acc[...] = jnp.zeros_like(q_acc)
-
     def second(b, total):
         rows = pl.ds(pl.multiple_of(b * BLOCK, BLOCK), BLOCK)
         part = jnp.exp2(logits[rows, :] - top)
         low = part.astype(BF16)
         raised[rows, :] = low
-        q_acc[...] += dot(code_t[:, rows], low)
         return total + jnp.sum(part.reshape(BLOCK // 8, 8, ROWS), axis=0)
 
     total = lax.fori_loop(0, BLOCKS, second, jnp.zeros((8, ROWS), F32))
     total = jnp.sum(total, axis=0, keepdims=True)
 
-    stat_in[xy, 0:1, :] = top
-    stat_in[xy, 1:2, :] = total
+    stat_in[xy] = top + jnp.log2(total)
     ends = (z == 0) | (z == LINE - 1)
 
     @pl.when(ends)
@@ -149,7 +144,7 @@
 
     each(lambda i: stat_copy(i).start())
 
-    q_send[...] = q_acc[...].astype(BF16)
+    q_send[...] = (dot(code_t[...], raised[...]) * (1.0 / total)).astype(BF16)
 
     def piece(j):
         return pl.ds(pl.multiple_of(j * PIECE, PIECE), PIECE)
@@ -168,35 +163,23 @@
     q_in[xy] = q_send[piece(xy), :]
 
     each(stat_wait)
-    plane_top = stat_in[0, 0:1, :]
+    plane_top = stat_in[0]
     for j in range(1, PLANE):
-        plane_top = jnp.maximum(plane_top, stat_in[j, 0:1, :])
+        plane_top = jnp.maximum(plane_top, stat_in[j])
     plane_total = jnp.zeros((1, ROWS), F32)
     for j in range(PLANE):
-        plane_total += stat_in[j, 1:2, :] * jnp.exp2(stat_in[j, 0:1, :] - plane_top)
-    zstat_out[0:1, :] = plane_top
-    zstat_out[1:2, :] = plane_total
+        plane_total += jnp.exp2(stat_in[j] - plane_top)
+    plane_log = plane_top + jnp.log2(plane_total)
+    zstat_out[...] = plane_log
     zstat_copy = pltpu.make_async_remote_copy(
         zstat_out, zstat_in, zstat_sem.at[0], zstat_sem.at[1], device_id=across, device_id_type=MESH)
     zstat_copy.start()
 
-    each(q_wait)
-    plane_q = jnp.zeros((PIECE, ROWS), F32)
-    for j in range(PLANE):
-        plane_q += q_in[j].astype(F32) * jnp.exp2(stat_in[j, 0:1, :] - plane_top)
-    zq_out[...] = plane_q.astype(BF16)
-    zq_copy = pltpu.make_async_remote_copy(
-        zq_out, zq_in, zq_sem.at[0], zq_sem.at[1], device_id=across, device_id_type=MESH)
-    zq_copy.start()
-
     zstat_copy.wait_recv()
-    other_top = zstat_in[0:1, :]
-    full_top = jnp.maximum(plane_top, other_top)
-    mine_factor = jnp.exp2(plane_top - full_top)
-    other_factor = jnp.exp2(other_top - full_top)
-    full_total = plane_total * mine_factor + zstat_in[1:2, :] * other_factor
-    inverse = 1.0 / full_total
-    factor = jnp.exp2(top - full_top) * inverse
+    other_log = zstat_in[...]
+    full_top = jnp.maximum(plane_log, other_log)
+    full_log = full_top + jnp.log2(jnp.exp2(plane_log - full_top) + jnp.exp2(other_log - full_top))
+    factor = jnp.exp2(top - full_log)
 
     for side in range(2):
         which = core if side == 0 else 1 - core
@@ -294,9 +277,19 @@
             cntp_copy.wait_recv()
             cnt_pair[...] += cnt[...]
 
+            each(q_wait)
+            plane_q = jnp.zeros((PIECE, ROWS), F32)
+            for j in range(PLANE):
+                plane_q += q_in[j].astype(F32) * jnp.exp2(stat_in[j] - full_log)
+            q_part[...] = plane_q
+            zq_out[...] = plane_q.astype(BF16)
+            zq_copy = pltpu.make_async_remote_copy(
+                zq_out, zq_in, zq_sem.at[0], zq_sem.at[1], device_id=across, device_id_type=MESH)
+            zq_copy.start()
+
+        if t == 3:
             zq_copy.wait_recv()
-            share_q = (plane_q * mine_factor + zq_in[...].astype(F32) * other_factor) * inverse
-            q_all[xy] = share_q.astype(BF16)
+            q_all[xy] = (q_part[...] + zq_in[...].astype(F32)).astype(BF16)
 
             def qa_copy(i):
                 j, device = peer(i)
@@ -329,7 +322,7 @@
             cntl_copy.start()
 
     each(qa_wait)
-    quant_ref[...] = q_all[...].reshape(WIDTH, ROWS).T
+    quant_ref[...] = q_all[...]
 
     @pl.when(z == 0)
     def _():
@@ -345,8 +338,6 @@
     def _():
         counts_ref[...] = cnt_pair[...] + cnt_left[...] + cnt_right[...]
 
-    counts_ref[...] = 0.9 * old_counts_ref[...] + 0.1 * counts_ref[...]
-
     for q in range(SUBS):
         @pl.when(z > 0)
         def _():
@@ -358,8 +349,7 @@
             left_copy(last - 1, q).wait_recv()
             own[share(z), sub(q)] += left_in[last - 1, :, sub(q)].astype(F32)
 
-        sums_next = 0.9 * old_sums_ref[:, sub(q)] + 0.1 * own[share(z), sub(q)]
-        next_ref[:, sub(q)] = sums_next / counts_ref[:, sub(q)]
+        sums_ref[:, sub(q)] = own[share(z), sub(q)]
 
     each(lambda i: stat_copy(i).wait_send())
     each(lambda i: q_copy(i).wait_send())
@@ -390,18 +380,25 @@
                 left_copy(t, q).wait_send()
 
 
+def finish(quant_t_ref, counts_ref, sums_ref, old_counts_ref, old_sums_ref, quant_ref, counts_next_ref, next_ref):
+    quant_ref[...] = quant_t_ref[...].reshape(WIDTH, ROWS).T
+    counts_next = 0.9 * old_counts_ref[...] + 0.1 * counts_ref[...]
+    counts_next_ref[...] = counts_next
+    next_ref[...] = (0.9 * old_sums_ref[...] + 0.1 * sums_ref[...]) / counts_next
+
+
 def body(latents, codebook, old_counts, old_sums):
     any_spec = pl.BlockSpec(memory_space=pl.ANY)
     vmem_spec = pl.BlockSpec(memory_space=pltpu.VMEM)
     dma = pltpu.SemaphoreType.DMA
-    quantized, counts_next, codebook_next = pl.pallas_call(
+    quant_t, counts, code_sums = pl.pallas_call(
         kernel,
         out_shape=(
-            jax.ShapeDtypeStruct((ROWS, WIDTH), BF16),
+            jax.ShapeDtypeStruct((PLANE, PIECE, ROWS), BF16),
             jax.ShapeDtypeStruct((1, CODES), F32),
             jax.ShapeDtypeStruct((SHARE, CODES), F32),
         ),
-        in_specs=[any_spec, any_spec, vmem_spec, vmem_spec],
+        in_specs=[any_spec, any_spec],
         out_specs=(vmem_spec, vmem_spec, vmem_spec),
         scratch_shapes=[
             pltpu.VMEM((ROWS, WIDTH), BF16),
@@ -410,10 +407,10 @@
             pltpu.VMEM((WIDTH, CODES), BF16),
             pltpu.VMEM((CODES, ROWS), F32),
             pltpu.VMEM((CODES, ROWS), BF16),
-            pltpu.VMEM((PLANE, 2, ROWS), F32),
-            pltpu.VMEM((2, ROWS), F32),
-            pltpu.VMEM((2, ROWS), F32),
-            pltpu.VMEM((WIDTH, ROWS), F32),
+            pltpu.VMEM((PLANE, 1, ROWS), F32),
+            pltpu.VMEM((1, ROWS), F32),
+            pltpu.VMEM((1, ROWS), F32),
+            pltpu.VMEM((PIECE, ROWS), F32),
             pltpu.VMEM((WIDTH, ROWS), BF16),
             pltpu.VMEM((PLANE, PIECE, ROWS), BF16),
             pltpu.VMEM((PIECE, ROWS), BF16),
@@ -456,7 +453,18 @@
         compiler_params=pltpu.CompilerParams(
             collective_id=0, has_side_effects=True, vmem_limit_bytes=60 * 1024 * 1024),
         cost_estimate=pl.CostEstimate(flops=6_500_000_000, bytes_accessed=4_000_000, transcendentals=4_200_000),
-    )(latents, codebook, old_counts.reshape(1, CODES), old_sums)
+    )(latents, codebook)
+    quantized, counts_next, codebook_next = pl.pallas_call(
+        finish,
+        out_shape=(
+            jax.ShapeDtypeStruct((ROWS, WIDTH), BF16),
+            jax.ShapeDtypeStruct((1, CODES), F32),
+            jax.ShapeDtypeStruct((SHARE, CODES), F32),
+        ),
+        in_specs=[vmem_spec] * 5,
+        out_specs=(vmem_spec, vmem_spec, vmem_spec),
+        cost_estimate=pl.CostEstimate(flops=300_000, bytes_accessed=2_000_000, transcendentals=0),
+    )(quant_t, counts, code_sums, old_counts.reshape(1, CODES), old_sums)
     return quantized, counts_next.reshape(CODES), codebook_next
 
 

time: 74.4 us -> 66.7 us (0.90)
  the two profiles are of different devices: /device:TPU:2 before, /device:TPU:32 now
where the time goes in v2:
time: 66.7 us; the launch traced here: 66.5 us
  Pallas kernels  65.9 us (99%)
    pallas_call x1, Pallas kernels, body(): pl.pallas_call(kernel, out_shape=(jax.ShapeDtypeStruct((PLANE, PIECE, ROW...  63.6 us
    pallas_call x1, Pallas kernels, body(): pl.pallas_call(finish, out_shape=(jax.ShapeDtypeStruct((ROWS, WIDTH), BF1...  2.32 us

profile of v2, /device:TPU:32, one launch (start us, length us, event | category | flops | bytes accessed | tf_op | source)
XLA Modules:
  0.0 66.5 jit_solution(4605822765863444443)
XLA Ops:
  0.6 63.6 %shard_map.67 = (bf16[16,16,1024]{2,1,0:T(8,128)(2,1)}, f32[1,4096]{1,0:T(1,128)}, f32[16,4096]{1,0:T(8,128)}) custom-call(bf16[1024,256]{1,0:T(8,128)(2,1)} %latents_hbm.1, bf16[4096,256]{1,0:T(8,128)(2,1)} %codebook_hbm.1), custom_call_target="tpu_custom_call" | custom-call | flops 6499999744 | bytes 4000000 | tf_op jit(solution)/shard_map/pallas_call | solution.py:394
  64.2 2.3 %shard_map.68 = (bf16[1024,256]{1,0:T(8,128)(2,1)}, f32[1,4096]{1,0:T(1,128)}, f32[16,4096]{1,0:T(8,128)}) custom-call(bf16[16,16,1024]{2,1,0:T(8,128)(2,1)} %get-tuple-element.9.quant_t_ref, f32[1,4096]{1,0:T(1,128)} %get-tuple-element.10.counts_ref, f32[16,4096]{1,0:T(8,128)} %get-tuple-element.11.sums_ref, f32[1,4096]{1,0:T(1,128)} %bitcast.2, ...), custom_call_target="tpu_custom_call" | custom-call | flops 300000 | bytes 2000000 | tf_op jit(solution)/shard_map/pallas_call | solution.py:457

commit v3 on v2

v3 whole, which is shorter than its diff:
```python
import math

import jax
import jax.numpy as jnp
from jax import lax
from jax.experimental import pallas as pl
from jax.experimental.pallas import tpu as pltpu
from jax.sharding import PartitionSpec as P

MESH = pl.DeviceIdType.MESH
F32 = jnp.float32
BF16 = jnp.bfloat16

ROWS = 1024
CODES = 4096
WIDTH = 256
BLOCK = 2048
BLOCKS = CODES // BLOCK
PLANE = 16
STRIP = ROWS // PLANE
PIECE = WIDTH // PLANE
LINE = 8
PART = CODES // 2
SUBS = 2
SUB = PART // SUBS
SHARE = 16
HALF = SHARE * LINE
QSTEP = 3
CSTEP = 3


def dot(a, b):
    return lax.dot_general(a, b, (((1,), (0,)), ((), ())), preferred_element_type=F32)


def dot_t(a, b):
    return lax.dot_general(a, b, (((1,), (1,)), ((), ())), preferred_element_type=F32)


def kernel(
    latents_hbm, codebook_hbm, quant_ref, counts_ref, sums_ref,
    lat, lat_t, lat2, lat2_t, code, code_t, logits, raised, raised2,
    stat_in, zstat_out, zstat_in,
    q_send, q_in, zq_out, zq_in, q_all,
    scaled, scaled2, own, pair_out, pair_in, cnt, cnt_pair, cnt_line, cnt_half,
    in_in, in_out, out_in, out_out, direct_in,
    lat_sem, code_sem, strip_s, strip_r, spread_s, spread_r,
    stat_s, stat_r, zstat_s, zstat_r, q_s, q_r, zq_sem, qa_s, qa_r,
    pair_s, pair_r, cntp_sem, cnt_s, cnt_r, half_sem, in_s, in_r, out_s, out_r, direct_r, ready,
):
    dp = lax.axis_index("dp")
    cd = lax.axis_index("code")
    z = dp // 2
    core = dp % 2
    zh = cd // PLANE
    xy = cd % PLANE
    partner = (dp + 1 - 2 * core, cd)
    cd_across = (1 - zh) * PLANE + xy
    across = (dp, cd_across)
    dp_pair = (dp + LINE) % (2 * LINE)
    part = z // 4
    place = z + part * (7 - 2 * z)
    relatives = (across, (dp_pair, cd), (dp_pair, cd_across))

    middle = ((4 - part) * 2 + core, cd)

    def mate(i):
        return ((part * 4 + (z + i) % 4) * 2 + core, cd)

    def peer(i):
        j = (xy + i) % PLANE
        return j, (dp, zh * PLANE + j)

    lat_copy = pltpu.make_async_copy(latents_hbm, lat, lat_sem)
    lat_copy.start()

    def code_copy(b):
        rows = pl.ds(pl.multiple_of(b * BLOCK, BLOCK), BLOCK)
        return pltpu.make_async_copy(codebook_hbm.at[rows], code.at[rows], code_sem.at[b])

    for b in range(BLOCKS):
        code_copy(b).start()

    barrier = pltpu.get_barrier_semaphore()

    def greet(i, carry):
        pl.semaphore_signal(barrier, inc=1, device_id=peer(i)[1], device_id_type=MESH)
        return carry

    lax.fori_loop(1, PLANE, greet, 0)
    greeted = [partner, (dp_pair, cd)] + [mate(i) for i in (1, 2, 3)]
    for device in greeted:
        pl.semaphore_signal(barrier, inc=1, device_id=device, device_id_type=MESH)

    @pl.when(place > 0)
    def _():
        pl.semaphore_signal(barrier, inc=1, device_id=middle, device_id_type=MESH)

    @pl.when(zh == 0)
    def _():
        for device in (across, (dp_pair, cd_across)):
            pl.semaphore_signal(barrier, inc=1, device_id=device, device_id_type=MESH)

    lat_copy.wait()
    lat_t[...] = lat[...].T
    per_dot = 2.0 * 2.0 / math.sqrt(WIDTH) * math.log2(math.e)
    per_norm = 2.0 / math.sqrt(WIDTH) * math.log2(math.e)

    def first(b, top):
        code_copy(b).wait()
        rows = pl.ds(pl.multiple_of(b * BLOCK, BLOCK), BLOCK)
        block = code[rows, :]
        wide = block.astype(F32)
        norms = jnp.sum(wide * wide, axis=1, keepdims=True) * per_norm
        part = dot(block, lat_t[...]) * per_dot - norms
        logits[rows, :] = part
        code_t[:, rows] = block.T
        return jnp.maximum(top, jnp.max(part.reshape(BLOCK // 8, 8, ROWS), axis=0))

    top = lax.fori_loop(0, BLOCKS, first, jnp.full((8, ROWS), -jnp.inf, F32))
    top = jnp.max(top, axis=0, keepdims=True)

    near = PLANE - 1 + 2 + 3
    for side in range(2):
        for mid in range(2):
            @pl.when((zh == side) & ((place == 3) == (mid == 1)))
            def _():
                pl.semaphore_wait(barrier, near + 2 * side + 3 * mid)

    @pl.when(zh == 1)
    def _():
        for device in (across, (dp_pair, cd_across)):
            pl.semaphore_signal(ready, inc=1, device_id=device, device_id_type=MESH)

    def strip(j):
        return pl.ds(pl.multiple_of(j * STRIP, STRIP), STRIP)

    strip_copy = pltpu.make_async_remote_copy(
        lat.at[strip(xy)], lat2.at[strip(xy)], strip_s, strip_r, device_id=(dp_pair, cd), device_id_type=MESH)
    strip_copy.start()

    def second(b, total):
        rows = pl.ds(pl.multiple_of(b * BLOCK, BLOCK), BLOCK)
        part = jnp.exp2(logits[rows, :] - top)
        low = part.astype(BF16)
        raised[rows, :] = low
        return total + jnp.sum(part.reshape(BLOCK // 8, 8, ROWS), axis=0)

    total = lax.fori_loop(0, BLOCKS, second, jnp.zeros((8, ROWS), F32))
    total = jnp.sum(total, axis=0, keepdims=True)

    stat_in[xy] = top + jnp.log2(total)
    def stat_copy(i):
        j, device = peer(i)
        return pltpu.make_async_remote_copy(
            stat_in.at[xy], stat_in.at[xy], stat_s.at[i], stat_r.at[xy], device_id=device, device_id_type=MESH)

    def stat_wait(i):
        j, device = peer(i)
        pltpu.make_async_remote_copy(
            stat_in.at[j], stat_in.at[j], stat_s.at[i], stat_r.at[j], device_id=device, device_id_type=MESH).wait_recv()

    def each(run):
        def step(i, carry):
            run(i)
            return carry
        lax.fori_loop(1, PLANE, step, 0)

    each(lambda i: stat_copy(i).start())

    q_send[...] = (dot(code_t[...], raised[...]) * (1.0 / total)).astype(BF16)

    def piece(j):
        return pl.ds(pl.multiple_of(j * PIECE, PIECE), PIECE)

    def q_copy(i):
        j, device = peer(i)
        return pltpu.make_async_remote_copy(
            q_send.at[piece(j)], q_in.at[xy], q_s.at[i], q_r.at[xy], device_id=device, device_id_type=MESH)

    def q_wait(i):
        j, device = peer(i)
        pltpu.make_async_remote_copy(
            q_send.at[piece(j)], q_in.at[j], q_s.at[i], q_r.at[j], device_id=device, device_id_type=MESH).wait_recv()

    def spread_copy(i):
        j, device = peer(i)
        return pltpu.make_async_remote_copy(
            lat2.at[strip(xy)], lat2.at[strip(xy)], spread_s.at[i], spread_r.at[xy], device_id=device, device_id_type=MESH)

    def spread_wait(i):
        j, device = peer(i)
        pltpu.make_async_remote_copy(
            lat2.at[strip(j)], lat2.at[strip(j)], spread_s.at[i], spread_r.at[j], device_id=device, device_id_type=MESH).wait_recv()

    each(lambda i: q_copy(i).start())
    strip_copy.wait_recv()
    each(lambda i: spread_copy(i).start())

    q_in[xy] = q_send[piece(xy), :]

    each(stat_wait)
    plane_top = stat_in[0]
    for j in range(1, PLANE):
        plane_top = jnp.maximum(plane_top, stat_in[j])
    plane_total = jnp.zeros((1, ROWS), F32)
    for j in range(PLANE):
        plane_total += jnp.exp2(stat_in[j] - plane_top)
    plane_log = plane_top + jnp.log2(plane_total)
    zstat_out[...] = plane_log

    def zstat_copy(k):
        return pltpu.make_async_remote_copy(
            zstat_out, zstat_in.at[k], zstat_s.at[k], zstat_r.at[k], device_id=relatives[k], device_id_type=MESH)

    @pl.when(zh == 0)
    def _():
        pl.semaphore_wait(ready, 2)

    for k in range(3):
        zstat_copy(k).start()

    each(q_wait)
    plane_q = jnp.zeros((PIECE, ROWS), F32)
    for j in range(PLANE):
        plane_q += q_in[j].astype(F32) * jnp.exp2(stat_in[j] - plane_log)
    zq_out[...] = plane_q.astype(BF16)
    zq_copy = pltpu.make_async_remote_copy(
        zq_out, zq_in, zq_sem.at[0], zq_sem.at[1], device_id=across, device_id_type=MESH)
    zq_copy.start()

    each(spread_wait)
    lat2_t[...] = lat2[...].T
    start = pl.multiple_of(part * PART, PART)
    block = code[pl.ds(start, PART), :]
    wide = block.astype(F32)
    norms = jnp.sum(wide * wide, axis=1, keepdims=True) * per_norm
    logits2 = dot(block, lat2_t[...]) * per_dot - norms
    logits[0:PART, :] = logits2
    top2 = jnp.max(jnp.max(logits2.reshape(PART // 8, 8, ROWS), axis=0), axis=0, keepdims=True)
    raised2[...] = jnp.exp2(logits[0:PART, :] - top2).astype(BF16)

    def log_sum(a, b):
        high = jnp.maximum(a, b)
        return high + jnp.log2(jnp.exp2(a - high) + jnp.exp2(b - high))

    for k in range(3):
        zstat_copy(k).wait_recv()
    full_log = log_sum(plane_log, zstat_in[0])
    factor = jnp.exp2(top - full_log)
    factor2 = jnp.exp2(top2 - log_sum(zstat_in[1], zstat_in[2]))

    line_no = lax.broadcasted_iota(jnp.int32, (SHARE, ROWS), 0)
    for out, rows_t, by in ((scaled, lat_t, factor), (scaled2, lat2_t, factor2)):
        for side in range(2):
            which = core if side == 0 else 1 - core
            for e in range(LINE):
                chip = e + part * (LINE - 1 - 2 * e)
                src = pl.ds(pl.multiple_of(chip * 2 * SHARE + which * SHARE, SHARE), SHARE)
                out[side * HALF + e * SHARE : side * HALF + (e + 1) * SHARE, :] = (
                    rows_t[src, :].astype(F32) * by).astype(BF16)
        high = by.astype(BF16).astype(F32)
        out[WIDTH : WIDTH + SHARE, :] = jnp.where(
            line_no == 0, high, jnp.where(line_no == 1, by - high, 0.0)).astype(BF16)

    def sub(q):
        return pl.ds(q * SUB, SUB)

    def pair_copy(q):
        return pltpu.make_async_remote_copy(
            pair_out.at[:, sub(q)], pair_in.at[:, sub(q)], pair_s.at[q], pair_r.at[q],
            device_id=partner, device_id_type=MESH)

    for q in range(SUBS):
        mine = pl.ds(pl.multiple_of(part * PART + q * SUB, SUB), SUB)
        sums = dot_t(scaled[...], raised[mine, :]) + dot_t(scaled2[...], raised2[sub(q), :])
        pair_out[:, sub(q)] = sums[HALF:WIDTH].astype(BF16)
        pair_copy(q).start()
        own[:, sub(q)] = sums[0:HALF]
        cnt[:, sub(q)] = sums[WIDTH : WIDTH + 1] + sums[WIDTH + 1 : WIDTH + 2]

    cntp_copy = pltpu.make_async_remote_copy(
        cnt, cnt_pair, cntp_sem.at[0], cntp_sem.at[1], device_id=partner, device_id_type=MESH)
    cntp_copy.start()

    toward = 2 * (1 - 2 * part)
    last = LINE - 1

    def in_copy(t, q):
        return pltpu.make_async_remote_copy(
            in_out.at[t, :, sub(q)], in_in.at[t, :, sub(q)], in_s.at[t, q], in_r.at[t, q],
            device_id=(dp + toward, cd), device_id_type=MESH)

    def direct_copy(t, q):
        e = 10 - t
        chip = e + part * (last - 2 * e)
        return pltpu.make_async_remote_copy(
            in_out.at[t, :, sub(q)], direct_in.at[:, sub(q)], in_s.at[t, q], direct_r.at[q],
            device_id=(chip * 2 + core, cd), device_id_type=MESH)

    def out_copy(t, q):
        return pltpu.make_async_remote_copy(
            out_out.at[t, :, sub(q)], out_in.at[t, :, sub(q)], out_s.at[t, q], out_r.at[t, q],
            device_id=(dp - toward, cd), device_id_type=MESH)

    def share(e):
        return pl.ds(pl.multiple_of(e * SHARE, SHARE), SHARE)

    def in_step(t, q):
        @pl.when(t >= place)
        def _():
            mine = own[share(last - t + place), sub(q)]

            @pl.when(place == 0)
            def _():
                in_out[t, :, sub(q)] = mine.astype(BF16)

            if t > 0:
                @pl.when(place > 0)
                def _():
                    in_copy(t - 1, q).wait_recv()
                    in_out[t, :, sub(q)] = (mine + in_in[t - 1, :, sub(q)].astype(F32)).astype(BF16)

            @pl.when(place < 3)
            def _():
                in_copy(t, q).start()

            if t >= 3:
                @pl.when(place == 3)
                def _():
                    direct_copy(t, q).start()

    def out_step(t, q):
        @pl.when((place > 0) & (t >= 3 - place))
        def _():
            mine = own[share(t - 3 + place), sub(q)]

            @pl.when(place == 3)
            def _():
                out_out[t, :, sub(q)] = mine.astype(BF16)

            if t > 0:
                @pl.when(place < 3)
                def _():
                    out_copy(t - 1, q).wait_recv()
                    out_out[t, :, sub(q)] = (mine + out_in[t - 1, :, sub(q)].astype(F32)).astype(BF16)

            out_copy(t, q).start()

    def cnt_copy(i):
        return pltpu.make_async_remote_copy(
            cnt_line.at[z % 4], cnt_line.at[z % 4], cnt_s.at[i], cnt_r.at[z % 4], device_id=mate(i), device_id_type=MESH)

    def cnt_wait(i):
        other = (z + i) % 4
        pltpu.make_async_remote_copy(
            cnt_line.at[other], cnt_line.at[other], cnt_s.at[i], cnt_r.at[other],
            device_id=mate(i), device_id_type=MESH).wait_recv()

    half_copy = pltpu.make_async_remote_copy(
        cnt_half.at[0], cnt_half.at[1], half_sem.at[0], half_sem.at[1], device_id=(dp_pair, cd), device_id_type=MESH)

    def qa_copy(i):
        j, device = peer(i)
        return pltpu.make_async_remote_copy(
            q_all.at[xy], q_all.at[xy], qa_s.at[i], qa_r.at[xy], device_id=device, device_id_type=MESH)

    def qa_wait(i):
        j, device = peer(i)
        pltpu.make_async_remote_copy(
            q_all.at[j], q_all.at[j], qa_s.at[i], qa_r.at[j], device_id=device, device_id_type=MESH).wait_recv()

    for t in range(last):
        for q in range(SUBS):
            if t == 0:
                pair_copy(q).wait_recv()
                own[:, sub(q)] += pair_in[:, sub(q)].astype(F32)
            in_step(t, q)
            if t < 3:
                out_step(t, q)
        if t == 0:
            cntp_copy.wait_recv()
            cnt_line[z % 4] = cnt_pair[...] + cnt[...]

            for i in range(1, 4):
                cnt_copy(i).start()

        if t == CSTEP:
            for i in range(1, 4):
                cnt_wait(i)
            cnt_half[0] = cnt_line[0] + cnt_line[1] + cnt_line[2] + cnt_line[3]
            half_copy.start()

        if t == QSTEP:
            zq_copy.wait_recv()
            q_all[xy] = (
                    zq_out[...].astype(F32) * jnp.exp2(plane_log - full_log)
                    + zq_in[...].astype(F32) * jnp.exp2(zstat_in[0] - full_log)).astype(BF16)
            each(lambda i: qa_copy(i).start())

    for q in range(SUBS):
        @pl.when(place > 0)
        def _():
            in_copy(last - 1, q).wait_recv()
            own[share(place), sub(q)] += in_in[last - 1, :, sub(q)].astype(F32)

        @pl.when(place < 3)
        def _():
            out_copy(2, q).wait_recv()
            own[share(place), sub(q)] += out_in[2, :, sub(q)].astype(F32)

        sums_ref[part, :, sub(q)] = own[share(place), sub(q)]

    for q in range(SUBS):
        pltpu.make_async_remote_copy(
            direct_in.at[:, sub(q)], direct_in.at[:, sub(q)], in_s.at[0, q], direct_r.at[q],
            device_id=partner, device_id_type=MESH).wait_recv()
        sums_ref[1 - part, :, sub(q)] = direct_in[:, sub(q)].astype(F32)

    half_copy.wait_recv()
    counts_ref[part] = cnt_half[0]
    counts_ref[1 - part] = cnt_half[1]
    each(qa_wait)
    quant_ref[...] = q_all[...]

    strip_copy.wait_send()
    each(lambda i: spread_copy(i).wait_send())
    each(lambda i: stat_copy(i).wait_send())
    each(lambda i: q_copy(i).wait_send())
    each(lambda i: qa_copy(i).wait_send())
    for k in range(3):
        zstat_copy(k).wait_send()
    zq_copy.wait_send()
    cntp_copy.wait_send()
    for i in range(1, 4):
        cnt_copy(i).wait_send()
    half_copy.wait_send()
    for q in range(SUBS):
        pair_copy(q).wait_send()
    for t in range(last):
        @pl.when(t >= place)
        def _():
            for q in range(SUBS):
                in_copy(t, q).wait_send()

        if t < 3:
            @pl.when((place > 0) & (t >= 3 - place))
            def _():
                for q in range(SUBS):
                    out_copy(t, q).wait_send()


def finish(quant_t_ref, counts_ref, sums_ref, old_counts_ref, old_sums_ref, quant_ref, counts_next_ref, next_ref):
    quant_ref[...] = quant_t_ref[...].reshape(WIDTH, ROWS).T
    for half in range(2):
        codes = pl.ds(half * PART, PART)
        counts_next = 0.9 * old_counts_ref[:, codes] + 0.1 * counts_ref[half]
        counts_next_ref[:, codes] = counts_next
        next_ref[:, codes] = (0.9 * old_sums_ref[:, codes] + 0.1 * sums_ref[half]) / counts_next


def body(latents, codebook, old_counts, old_sums):
    any_spec = pl.BlockSpec(memory_space=pl.ANY)
    vmem_spec = pl.BlockSpec(memory_space=pltpu.VMEM)
    dma = pltpu.SemaphoreType.DMA
    quant_t, counts, code_sums = pl.pallas_call(
        kernel,
        out_shape=(
            jax.ShapeDtypeStruct((PLANE, PIECE, ROWS), BF16),
            jax.ShapeDtypeStruct((2, 1, PART), F32),
            jax.ShapeDtypeStruct((2, SHARE, PART), F32),
        ),
        in_specs=[any_spec, any_spec],
        out_specs=(vmem_spec, vmem_spec, vmem_spec),
        scratch_shapes=[
            pltpu.VMEM((ROWS, WIDTH), BF16),
            pltpu.VMEM((WIDTH, ROWS), BF16),
            pltpu.VMEM((ROWS, WIDTH), BF16),
            pltpu.VMEM((WIDTH, ROWS), BF16),
            pltpu.VMEM((CODES, WIDTH), BF16),
            pltpu.VMEM((WIDTH, CODES), BF16),
            pltpu.VMEM((CODES, ROWS), F32),
            pltpu.VMEM((CODES, ROWS), BF16),
            pltpu.VMEM((PART, ROWS), BF16),
            pltpu.VMEM((PLANE, 1, ROWS), F32),
            pltpu.VMEM((1, ROWS), F32),
            pltpu.VMEM((3, 1, ROWS), F32),
            pltpu.VMEM((WIDTH, ROWS), BF16),
            pltpu.VMEM((PLANE, PIECE, ROWS), BF16),
            pltpu.VMEM((PIECE, ROWS), BF16),
            pltpu.VMEM((PIECE, ROWS), BF16),
            pltpu.VMEM((PLANE, PIECE, ROWS), BF16),
            pltpu.VMEM((WIDTH + SHARE, ROWS), BF16),
            pltpu.VMEM((WIDTH + SHARE, ROWS), BF16),
            pltpu.VMEM((HALF, PART), F32),
            pltpu.VMEM((HALF, PART), BF16),
            pltpu.VMEM((HALF, PART), BF16),
            pltpu.VMEM((1, PART), F32),
            pltpu.VMEM((1, PART), F32),
            pltpu.VMEM((4, 1, PART), F32),
            pltpu.VMEM((2, 1, PART), F32),
            pltpu.VMEM((LINE - 1, SHARE, PART), BF16),
            pltpu.VMEM((LINE - 1, SHARE, PART), BF16),
            pltpu.VMEM((3, SHARE, PART), BF16),
            pltpu.VMEM((3, SHARE, PART), BF16),
            pltpu.VMEM((SHARE, PART), BF16),
            dma,
            dma((BLOCKS,)),
            dma,
            dma,
            dma((PLANE,)),
            dma((PLANE,)),
            dma((PLANE,)),
            dma((PLANE,)),
            dma((3,)),
            dma((3,)),
            dma((PLANE,)),
            dma((PLANE,)),
            dma((2,)),
            dma((PLANE,)),
            dma((PLANE,)),
            dma((SUBS,)),
            dma((SUBS,)),
            dma((2,)),
            dma((4,)),
            dma((4,)),
            dma((2,)),
            dma((LINE - 1, SUBS)),
            dma((LINE - 1, SUBS)),
            dma((3, SUBS)),
            dma((3, SUBS)),
            dma((SUBS,)),
            pltpu.SemaphoreType.REGULAR,
        ],
        compiler_params=pltpu.CompilerParams(
            collective_id=0, has_side_effects=True, vmem_limit_bytes=60 * 1024 * 1024),
        cost_estimate=pl.CostEstimate(flops=6_500_000_000, bytes_accessed=4_000_000, transcendentals=4_200_000),
    )(latents, codebook)
    quantized, counts_next, codebook_next = pl.pallas_call(
        finish,
        out_shape=(
            jax.ShapeDtypeStruct((ROWS, WIDTH), BF16),
            jax.ShapeDtypeStruct((1, CODES), F32),
            jax.ShapeDtypeStruct((SHARE, CODES), F32),
        ),
        in_specs=[vmem_spec] * 5,
        out_specs=(vmem_spec, vmem_spec, vmem_spec),
        cost_estimate=pl.CostEstimate(flops=300_000, bytes_accessed=2_000_000, transcendentals=0),
    )(quant_t, counts, code_sums, old_counts.reshape(1, CODES), old_sums)
    return quantized, counts_next.reshape(CODES), codebook_next


def solution(mesh):
    return jax.shard_map(
        body,
        mesh=mesh,
        in_specs=(P("dp", None), P("code", None), P("code"), P("dp", "code")),
        out_specs=(P("dp", None), P("code"), P("dp", "code")),
        check_vma=False,
    )
```

time: 66.7 us -> 60.1 us (0.901)
  the two profiles are of different devices: /device:TPU:32 before, /device:TPU:70 now
where the time goes in v3:
time: 60.1 us; the launch traced here: 60 us
  Pallas kernels  59.3 us (99%)
  between operations  0.64 us (1%)
    pallas_call x1, Pallas kernels, body(): pl.pallas_call(kernel, out_shape=(jax.ShapeDtypeStruct((PLANE, PIECE, ROW...  57 us
    pallas_call x1, Pallas kernels, body(): pl.pallas_call(finish, out_shape=(jax.ShapeDtypeStruct((ROWS, WIDTH), BF1...  2.31 us

profile of v3, /device:TPU:70, one launch (start us, length us, event | category | flops | bytes accessed | tf_op | source)
XLA Modules:
  0.0 60.0 jit_solution(16883866522099318478)
XLA Ops:
  0.6 57.0 %shard_map.67 = (bf16[16,16,1024]{2,1,0:T(8,128)(2,1)}, f32[2,1,2048]{2,1,0:T(1,128)}, f32[2,16,2048]{2,1,0:T(8,128)}) custom-call(bf16[1024,256]{1,0:T(8,128)(2,1)} %latents_hbm.1, bf16[4096,256]{1,0:T(8,128)(2,1)} %codebook_hbm.1), custom_call_target="tpu_custom_call" | custom-call | flops 6499999744 | bytes 4000000 | tf_op jit(solution)/shard_map/pallas_call | solution.py:466
  57.6 2.3 %shard_map.68 = (bf16[1024,256]{1,0:T(8,128)(2,1)}, f32[1,4096]{1,0:T(1,128)}, f32[16,4096]{1,0:T(8,128)}) custom-call(bf16[16,16,1024]{2,1,0:T(8,128)(2,1)} %get-tuple-element.9.quant_t_ref, f32[2,1,2048]{2,1,0:T(1,128)} %get-tuple-element.10.counts_ref, f32[2,16,2048]{2,1,0:T(8,128)} %get-tuple-element.11.sums_ref, f32[1,4096]{1,0:T(1,128)} %bitcast.2, ...), custom_call_target="tpu_custom_call" | custom-call | flops 300000 | bytes 2000000 | tf_op jit(solution)/shard_map/pallas_call | solution.py:539

commit v4 on v3

--- a/solution.py
+++ b/solution.py
@@ -17,6 +17,7 @@
 BLOCK = 2048
 BLOCKS = CODES // BLOCK
 PLANE = 16
+GROUP = ROWS // 4
 STRIP = ROWS // PLANE
 PIECE = WIDTH // PLANE
 LINE = 8
@@ -25,8 +26,7 @@
 SUB = PART // SUBS
 SHARE = 16
 HALF = SHARE * LINE
-QSTEP = 3
-CSTEP = 3
+GSTEP = 1
 
 
 def dot(a, b):
@@ -42,7 +42,7 @@
     lat, lat_t, lat2, lat2_t, code, code_t, logits, raised, raised2,
     stat_in, zstat_out, zstat_in,
     q_send, q_in, zq_out, zq_in, q_all,
-    scaled, scaled2, own, pair_out, pair_in, cnt, cnt_pair, cnt_line, cnt_half,
+    norms2, top2_ref, scaled, scaled2, own, pair_out, pair_in, cnt, cnt_pair, cnt_line, cnt_half,
     in_in, in_out, out_in, out_out, direct_in,
     lat_sem, code_sem, strip_s, strip_r, spread_s, spread_r,
     stat_s, stat_r, zstat_s, zstat_r, q_s, q_r, zq_sem, qa_s, qa_r,
@@ -188,14 +188,12 @@
         return pltpu.make_async_remote_copy(
             lat2.at[strip(xy)], lat2.at[strip(xy)], spread_s.at[i], spread_r.at[xy], device_id=device, device_id_type=MESH)
 
-    def spread_wait(i):
-        j, device = peer(i)
-        pltpu.make_async_remote_copy(
-            lat2.at[strip(j)], lat2.at[strip(j)], spread_s.at[i], spread_r.at[j], device_id=device, device_id_type=MESH).wait_recv()
-
-    each(lambda i: q_copy(i).start())
     strip_copy.wait_recv()
     each(lambda i: spread_copy(i).start())
+    @pl.when(core == 0)
+    def _():
+        each(lambda i: q_copy(i).start())
+
 
     q_in[xy] = q_send[piece(xy), :]
 
@@ -220,25 +218,40 @@
     for k in range(3):
         zstat_copy(k).start()
 
-    each(q_wait)
-    plane_q = jnp.zeros((PIECE, ROWS), F32)
-    for j in range(PLANE):
-        plane_q += q_in[j].astype(F32) * jnp.exp2(stat_in[j] - plane_log)
-    zq_out[...] = plane_q.astype(BF16)
-    zq_copy = pltpu.make_async_remote_copy(
-        zq_out, zq_in, zq_sem.at[0], zq_sem.at[1], device_id=across, device_id_type=MESH)
-    zq_copy.start()
-
-    each(spread_wait)
-    lat2_t[...] = lat2[...].T
     start = pl.multiple_of(part * PART, PART)
-    block = code[pl.ds(start, PART), :]
-    wide = block.astype(F32)
-    norms = jnp.sum(wide * wide, axis=1, keepdims=True) * per_norm
-    logits2 = dot(block, lat2_t[...]) * per_dot - norms
-    logits[0:PART, :] = logits2
-    top2 = jnp.max(jnp.max(logits2.reshape(PART // 8, 8, ROWS), axis=0), axis=0, keepdims=True)
-    raised2[...] = jnp.exp2(logits[0:PART, :] - top2).astype(BF16)
+    wide = code[pl.ds(start, PART), :].astype(F32)
+    norms2[...] = jnp.sum(wide * wide, axis=1, keepdims=True) * per_norm
+
+    def again(g, carry):
+        group = (xy // 4 + g) % 4
+
+        def arrive(i, carry):
+            j = group * 4 + i
+
+            @pl.when(j != xy)
+            def _():
+                pltpu.make_async_remote_copy(
+                    lat2.at[strip(j)], lat2.at[strip(j)], spread_s.at[i], spread_r.at[j],
+                    device_id=partner, device_id_type=MESH).wait_recv()
+            return carry
+
+        lax.fori_loop(0, 4, arrive, 0)
+        some = pl.ds(pl.multiple_of(group * GROUP, GROUP), GROUP)
+        lat2_t[:, some] = lat2[some, :].T
+        logits2 = dot(code[pl.ds(start, PART), :], lat2_t[:, some]) * per_dot - norms2[...]
+        logits[0:PART, 0:GROUP] = logits2
+        high = jnp.max(jnp.max(logits2.reshape(PART // 8, 8, GROUP), axis=0), axis=0, keepdims=True)
+        top2_ref[:, some] = high
+        raised2[:, some] = jnp.exp2(logits[0:PART, 0:GROUP] - high).astype(BF16)
+
+        @pl.when((core == 1) & (g == GSTEP))
+        def _():
+            each(lambda i: q_copy(i).start())
+
+        return carry
+
+    lax.fori_loop(0, 4, again, 0)
+    top2 = top2_ref[...]
 
     def log_sum(a, b):
         high = jnp.maximum(a, b)
@@ -283,6 +296,15 @@
         cnt, cnt_pair, cntp_sem.at[0], cntp_sem.at[1], device_id=partner, device_id_type=MESH)
     cntp_copy.start()
 
+    each(q_wait)
+    plane_q = jnp.zeros((PIECE, ROWS), F32)
+    for j in range(PLANE):
+        plane_q += q_in[j].astype(F32) * jnp.exp2(stat_in[j] - plane_log)
+    zq_out[...] = plane_q.astype(BF16)
+    zq_copy = pltpu.make_async_remote_copy(
+        zq_out, zq_in, zq_sem.at[0], zq_sem.at[1], device_id=across, device_id_type=MESH)
+    zq_copy.start()
+
     toward = 2 * (1 - 2 * part)
     last = LINE - 1
 
@@ -385,18 +407,19 @@
             for i in range(1, 4):
                 cnt_copy(i).start()
 
-        if t == CSTEP:
-            for i in range(1, 4):
-                cnt_wait(i)
-            cnt_half[0] = cnt_line[0] + cnt_line[1] + cnt_line[2] + cnt_line[3]
-            half_copy.start()
-
-        if t == QSTEP:
-            zq_copy.wait_recv()
-            q_all[xy] = (
-                    zq_out[...].astype(F32) * jnp.exp2(plane_log - full_log)
-                    + zq_in[...].astype(F32) * jnp.exp2(zstat_in[0] - full_log)).astype(BF16)
-            each(lambda i: qa_copy(i).start())
+        if t in (2, last - 1):
+            @pl.when((place == 0) == (t == last - 1))
+            def _():
+                for i in range(1, 4):
+                    cnt_wait(i)
+                cnt_half[0] = cnt_line[0] + cnt_line[1] + cnt_line[2] + cnt_line[3]
+                half_copy.start()
+
+                zq_copy.wait_recv()
+                q_all[xy] = (
+                        zq_out[...].astype(F32) * jnp.exp2(plane_log - full_log)
+                        + zq_in[...].astype(F32) * jnp.exp2(zstat_in[0] - full_log)).astype(BF16)
+                each(lambda i: qa_copy(i).start())
 
     for q in range(SUBS):
         @pl.when(place > 0)
@@ -490,6 +513,8 @@
             pltpu.VMEM((PIECE, ROWS), BF16),
             pltpu.VMEM((PIECE, ROWS), BF16),
             pltpu.VMEM((PLANE, PIECE, ROWS), BF16),
+            pltpu.VMEM((PART, 1), F32),
+            pltpu.VMEM((1, ROWS), F32),
             pltpu.VMEM((WIDTH + SHARE, ROWS), BF16),
             pltpu.VMEM((WIDTH + SHARE, ROWS), BF16),
             pltpu.VMEM((HALF, PART), F32),

time: 60.1 us -> 58.9 us (0.980)
  the two profiles are of different devices: /device:TPU:70 before, /device:TPU:96 now
where the time goes in v4:
time: 58.9 us; the launch traced here: 58.7 us
  Pallas kernels  58 us (98%)
  between operations  0.64 us (1%)
    pallas_call x1, Pallas kernels, body(): pl.pallas_call(kernel, out_shape=(jax.ShapeDtypeStruct((PLANE, PIECE, ROW...  55.7 us
    pallas_call x1, Pallas kernels, body(): pl.pallas_call(finish, out_shape=(jax.ShapeDtypeStruct((ROWS, WIDTH), BF1...  2.31 us

profile of v4, /device:TPU:96, one launch (start us, length us, event | category | flops | bytes accessed | tf_op | source)
XLA Modules:
  0.0 58.7 jit_solution(13074777334650718620)
XLA Ops:
  0.6 55.7 %shard_map.67 = (bf16[16,16,1024]{2,1,0:T(8,128)(2,1)}, f32[2,1,2048]{2,1,0:T(1,128)}, f32[2,16,2048]{2,1,0:T(8,128)}) custom-call(bf16[1024,256]{1,0:T(8,128)(2,1)} %latents_hbm.1, bf16[4096,256]{1,0:T(8,128)(2,1)} %codebook_hbm.1), custom_call_target="tpu_custom_call" | custom-call | flops 6499999744 | bytes 4000000 | tf_op jit(solution)/shard_map/pallas_call | solution.py:489
  56.4 2.3 %shard_map.68 = (bf16[1024,256]{1,0:T(8,128)(2,1)}, f32[1,4096]{1,0:T(1,128)}, f32[16,4096]{1,0:T(8,128)}) custom-call(bf16[16,16,1024]{2,1,0:T(8,128)(2,1)} %get-tuple-element.9.quant_t_ref, f32[2,1,2048]{2,1,0:T(1,128)} %get-tuple-element.10.counts_ref, f32[2,16,2048]{2,1,0:T(8,128)} %get-tuple-element.11.sums_ref, f32[1,4096]{1,0:T(1,128)} %bitcast.2, ...), custom_call_target="tpu_custom_call" | custom-call | flops 300000 | bytes 2000000 | tf_op jit(solution)/shard_map/pallas_call | solution.py:564

commit v5 on v4

--- a/solution.py
+++ b/solution.py
@@ -22,7 +22,7 @@
 PIECE = WIDTH // PLANE
 LINE = 8
 PART = CODES // 2
-SUBS = 2
+SUBS = 4
 SUB = PART // SUBS
 SHARE = 16
 HALF = SHARE * LINE

time: 58.9 us -> 58.5 us (level)
  no operation moved by 1% of the time
where the time goes in v5:
time: 58.5 us; the launch traced here: 58.3 us
  Pallas kernels  57.7 us (99%)
  between operations  0.64 us (1%)
    pallas_call x1, Pallas kernels, body(): pl.pallas_call(kernel, out_shape=(jax.ShapeDtypeStruct((PLANE, PIECE, ROW...  55.4 us
    pallas_call x1, Pallas kernels, body(): pl.pallas_call(finish, out_shape=(jax.ShapeDtypeStruct((ROWS, WIDTH), BF1...  2.31 us

profile of v5, /device:TPU:96, one launch (start us, length us, event | category | flops | bytes accessed | tf_op | source)
XLA Modules:
  0.0 58.3 jit_solution(4284330292461076869)
XLA Ops:
  0.6 55.4 %shard_map.67 = (bf16[16,16,1024]{2,1,0:T(8,128)(2,1)}, f32[2,1,2048]{2,1,0:T(1,128)}, f32[2,16,2048]{2,1,0:T(8,128)}) custom-call(bf16[1024,256]{1,0:T(8,128)(2,1)} %latents_hbm.1, bf16[4096,256]{1,0:T(8,128)(2,1)} %codebook_hbm.1), custom_call_target="tpu_custom_call" | custom-call | flops 6499999744 | bytes 4000000 | tf_op jit(solution)/shard_map/pallas_call | solution.py:489
  56.0 2.3 %shard_map.68 = (bf16[1024,256]{1,0:T(8,128)(2,1)}, f32[1,4096]{1,0:T(1,128)}, f32[16,4096]{1,0:T(8,128)}) custom-call(bf16[16,16,1024]{2,1,0:T(8,128)(2,1)} %get-tuple-element.9.quant_t_ref, f32[2,1,2048]{2,1,0:T(1,128)} %get-tuple-element.10.counts_ref, f32[2,16,2048]{2,1,0:T(8,128)} %get-tuple-element.11.sums_ref, f32[1,4096]{1,0:T(1,128)} %bitcast.2, ...), custom_call_target="tpu_custom_call" | custom-call | flops 300000 | bytes 2000000 | tf_op jit(solution)/shard_map/pallas_call | solution.py:564
